TPU v7x, 32 devices: a whole 2x2x4 slice. The times are simulated.
32 devices in a mesh: blk: 8 (over z, y), gy: 4 (over x, core).
Axes of the slice: x: 2, y: 2, z: 4, core: 2. Of those that a mesh axis runs over, the one named last changes fastest.
Arguments:
- image: float32 [1, 2048, 2048], P(None, 'blk', 'gy'), may hold values from -6 to 6
- measured: float32 [1, 16, 2816], P(None, 'blk'), may hold values from -6 to 6
- row_weight: float32 [16, 2816], P('blk'), may hold values from 0.25 to 2
- col_weight: float32 [2048, 2048], P('blk', 'gy'), may hold values from 1 to 8
- band_weight: bfloat16 [16, 2048, 128], P('blk', 'gy'), may hold values from -0.01171875 to 0.01171875
- band_shift: int32 [16, 8], replicated, may hold values from 0 to 3
Outputs:
- updated: float32 [1, 2048, 2048], P(None, 'blk', 'gy')
Inputs may be any that keep to these rules, and one draw needn't show every extreme that they name: band_shift[t, s] is the number of panels by which slab s's footprint under tilt t starts beyond panel s * 2.
All inputs are finite; a program needn't handle non-finite values.
Results may differ from a plain program's by a relative error of at most 0.0025.
Values may be sent and summed in bfloat16 or wider, within the bound.
A program may use at most 64 MiB of HBM per device.

v0:
```python
import math
import jax
import jax.numpy as jnp
from jax import lax
from jax.sharding import PartitionSpec as P

PW = 128
SMOOTH = 0.25


def with_halo(cells, sides, width):
    for axis, dim in sides:
        count = lax.axis_size(axis)
        ends = count - 1
        head = lax.slice_in_dim(cells, 0, width, axis=dim)
        tail = lax.slice_in_dim(cells, cells.shape[dim] - width, cells.shape[dim], axis=dim)
        cells = jnp.concatenate(
            [
                lax.ppermute(tail, axis, [(i, (i + 1) % count) for i in range(ends)]),
                cells,
                lax.ppermute(head, axis, [((i + 1) % count, i) for i in range(ends)]),
            ],
            axis=dim,
        )
    return cells


def shift_rows(rows, direction):
    col_count = rows.shape[-2]
    bit_count = (col_count - 1).bit_length()
    column_index = jnp.arange(col_count, dtype=jnp.int32)[:, None]
    for level in range(bit_count):
        moved = jnp.roll(rows, direction * (1 << level), axis=-1)
        chosen = column_index >> level & 1 == 1
        rows = jnp.where(chosen, moved, rows)
    return rows


def diagonal_sum(product):
    leading = product.shape[:-2]
    col_count, band_width = product.shape[-2:]
    keep_pads = [(0, 0)] * (len(leading) + 1)
    padded = jnp.pad(product, keep_pads + [(0, col_count)])
    return jnp.sum(shift_rows(padded, 1), axis=-2)


def band_rows(panels, col_count, band_width):
    leading = panels.shape[:-1]
    window_len = panels.shape[-1]
    repeated = jnp.broadcast_to(panels[..., None, :], leading + (col_count, window_len))
    return shift_rows(repeated, -1)[..., :band_width]


def per_device(image, measured, row_weight, col_weight, band_weight, band_shift):
    row_count, col_count, depth_count = image.shape
    local_tilts = measured.shape[1]
    detector_len = measured.shape[2]
    band_width = band_weight.shape[2]
    window_len = col_count + band_width
    block_count = lax.axis_size("blk")
    myself = lax.axis_index("blk")
    tilt_count = local_tilts * block_count
    per_slab = col_count // PW
    zero_index = jnp.int32(0)
    copies = image.astype(jnp.bfloat16)
    slab_bins = ((jnp.arange(block_count, dtype=jnp.int32) * per_slab)[None, :] + band_shift) * PW
    first_tilt = myself * local_tilts
    own_bins = lax.dynamic_slice_in_dim(slab_bins, first_tilt, local_tilts, 0)
    group_size = math.gcd(tilt_count, 8)
    all_weights = lax.all_gather(band_weight, "blk", axis=0, tiled=True)
    weight_groups = all_weights.reshape(
        tilt_count // group_size, group_size, depth_count, band_width
    )

    def place_windows(running, windows, source):
        for tilt_slot in range(local_tilts):
            offset = own_bins[tilt_slot, source]
            corner = (zero_index, jnp.int32(tilt_slot), offset)
            current = lax.dynamic_slice(running, corner, (row_count, 1, window_len))
            running = lax.dynamic_update_slice(
                running, current + windows[tilt_slot][:, None, :], corner
            )
        return running

    initial = jnp.zeros((row_count, local_tilts, detector_len), jnp.float32)

    def project_group(weights):
        product = jnp.einsum("yiz,tzd->tyid", copies, weights, preferred_element_type=jnp.float32)
        return diagonal_sum(product)

    windows = lax.map(project_group, weight_groups)
    windows = windows.reshape(block_count, local_tilts, row_count, window_len)
    received = lax.all_to_all(windows, "blk", split_axis=0, concat_axis=0, tiled=True)

    def add_source(source, running):
        return place_windows(
            running, lax.dynamic_index_in_dim(received, source, 0, keepdims=False), source
        )

    partial_sum = lax.fori_loop(0, block_count, add_source, initial)
    projection = lax.psum(partial_sum, "gy")
    weighted = (row_weight[None] * (measured - projection)).astype(jnp.bfloat16)

    def cut_panels(slab_offsets):
        pieces = [
            lax.dynamic_slice(
                weighted[:, tilt_slot],
                (zero_index, slab_offsets[tilt_slot]),
                (row_count, window_len),
            )
            for tilt_slot in range(local_tilts)
        ]
        return jnp.stack(pieces, axis=1)

    outgoing = jax.vmap(cut_panels, in_axes=1, out_axes=1)(own_bins)
    arrived = lax.all_to_all(outgoing, "blk", split_axis=1, concat_axis=1, tiled=True)
    panels = arrived.reshape(row_count, tilt_count, window_len)
    panel_groups = panels.reshape(
        row_count, tilt_count // group_size, group_size, window_len
    ).transpose(1, 0, 2, 3)

    def back_group(running, operands):
        panel_part, weight_part = operands
        sheared = band_rows(panel_part, col_count, band_width)
        added = jnp.einsum(
            "ytid,tzd->yiz", sheared, weight_part, preferred_element_type=jnp.float32
        )
        return (running + added, None)

    start_back = jnp.zeros((row_count, col_count, depth_count), jnp.float32)
    backed, leftover = lax.scan(back_group, start_back, (panel_groups, weight_groups))
    padded_depth = with_halo(image.astype(jnp.bfloat16), (("gy", 2),), 1).astype(image.dtype)
    return (
        image
        + col_weight[None] * backed
        + SMOOTH * (padded_depth[:, :, :-2] + padded_depth[:, :, 2:] - 2.0 * image)
    )


def solution(mesh):
    return jax.shard_map(
        per_device,
        mesh=mesh,
        in_specs=(
            P(None, "blk", "gy"),
            P(None, "blk", None),
            P("blk", None),
            P("blk", "gy"),
            P("blk", "gy", None),
            P(),
        ),
        out_specs=P(None, "blk", "gy"),
        check_vma=False,
    )
```

profile of v0, /device:TPU:0, one launch (start us, length us, event | category | flops | bytes accessed | tf_op | source)
XLA Modules:
  0.0 203.8 jit_solution(14922307778124006677)
XLA Ops:
  7.3 1.1 convert_element_type.22
  9.0 3.0 %collective-permute-start = (bf16[1,256,1]{2,1,0:T(8,128)(2,1)}, bf16[1,256,1]{2,1,0:T(8,128)(2,1)}, u32[]{:S(2)}, u32[]{:S(2)}) collective-permute-start(bf16[1,256,1]{2,1,0:T(8,128)(2,1)} %get-tuple-element.283), channel_id=1, source_target_pairs={{0,1},{1,2},{2,3},{4,5},{5,6},{6,7},{8,9},{9,10},{10,11},{12,13},{... | collective-permute-start | bytes 1544 | tf_op jit(solution)/shard_map/ppermute | solution.py:19
  12.0 1.3 collective-permute-start.1
  15.5 46.0 %all-gather.2.cloned.1.call-done = bf16[16,512,128]{2,1,0:T(8,128)(2,1)} async-done(((bf16[2,512,128]{2,1,0:T(8,128)(2,1)}), bf16[16,512,128]{2,1,0:T(8,128)(2,1)}) %all-gather.2.cloned.1.call-update) | async-done | bytes 2097168 | tf_op jit(solution)/shard_map/all_gather | solution.py:70
  61.5 14.9 %while.38 = (s32[]{:T(128)}, f32[2,8,1,384]{3,2,1,0:T(1,128)}, bf16[2,8,512,128]{3,2,1,0:T(8,128)(2,1)}, bf16[1,256,512]{2,1,0:T(8,128)(2,1)S(1)}, s32[]{:T(128)}) while((s32[]{:T(128)}, f32[2,8,1,384]{3,2,1,0:T(1,128)}, bf16[2,8,512,128]{3,2,1,0:T(8,128)(2,1)}, bf16[1,256,512]{2,1,0:T(8,128)(2,1)S(1)}, s32[]{:T(128)}) %tuple.126), condition=%wide.region_2.3_spmd, body=%wide.region_0.2_spmd.sunk | while | flops 281021440 | bytes 108389440 | solution.py:91
  61.5 1.7 convolution_bitcast_fusion.3
  69.0 1.7 convolution_bitcast_fusion.3
  76.4 3.3 %all-to-all-start = ((f32[8,2,1,384]{3,2,1,0:T(1,128)}), f32[8,2,1,384]{3,2,1,0:T(1,128)S(1)}, u32[]{:S(2)}, u32[]{:S(2)}) async-start(f32[8,2,1,384]{3,2,1,0:T(1,128)} %bitcast.12), calls=%async_computation | async-start | bytes 49152 | tf_op jit(solution)/shard_map/all_to_all | solution.py:93
  79.9 6.4 %all-to-all-done = f32[8,2,1,384]{3,2,1,0:T(1,128)S(1)} async-done(((f32[8,2,1,384]{3,2,1,0:T(1,128)}), f32[8,2,1,384]{3,2,1,0:T(1,128)S(1)}, u32[]{:S(2)}, u32[]{:S(2)}) %all-to-all-start) | async-done | bytes 24608 | tf_op jit(solution)/shard_map/all_to_all | solution.py:93
  86.3 35.3 %while.39 = (s32[]{:T(128)}, f32[1,2,2816]{2,1,0:T(2,128)S(1)}, s32[2,8]{1,0:T(2,128)S(1)}, f32[8,2,1,384]{3,2,1,0:T(1,128)S(1)}, s32[]{:T(128)}, /*index=5*/s32[]{:T(128)}, s32[]{:T(128)}, s32[]{}) while((s32[]{:T(128)}, f32[1,2,2816]{2,1,0:T(2,128)S(1)}, s32[2,8]{1,0:T(2,128)S(1)}, f32[8,2,1,384]{3,2,1,0:T(1,128)S(1)}, s32[]{:T(128)}, ...), condition=%wide.region_4.5_spmd, body=%wide.region_3.4_spmd.sunk | while | flops 777 | bytes 15573 | solution.py:100
  121.7 10.3 %psum.7 = f32[1,2,2816]{2,1,0:T(2,128)S(1)} all-reduce(f32[1,2,2816]{2,1,0:T(2,128)S(1)} %get-tuple-element.160), channel_id=1, replica_groups=mesh['blk'=8,'gy'=4] {'gy'}, use_global_device_ids=true, to_apply=%region_5.6 | all-reduce | flops 5632 | bytes 45056 | tf_op jit(solution)/shard_map/psum | solution.py:101
  132.0 11.8 %while.40 = (s32[]{:T(128)}, bf16[1,2816]{1,0:T(2,128)(2,1)S(1)}, s32[8,2]{0,1:T(2,128)S(1)}, bf16[8,1,384]{2,0,1:T(8,128)(2,1)S(1)}, s32[]{:T(128)}, /*index=5*/s32[]{:T(128)}) while((s32[]{:T(128)}, bf16[1,2816]{1,0:T(2,128)(2,1)S(1)}, s32[8,2]{0,1:T(2,128)S(1)}, bf16[8,1,384]{2,0,1:T(8,128)(2,1)S(1)}, s32[]{:T(128)}, /*index=5*/s32[]{:T(128)}) %tuple.118), condition=%wide.while_cond, body=%wide.while_body.sunk | while | flops 2 | bytes 3177 | solution.py:106
  143.9 10.7 %while.41 = (s32[]{:T(128)}, bf16[1,2816]{1,0:T(2,128)(2,1)S(1)}, s32[8,2]{0,1:T(2,128)S(1)}, bf16[8,1,384]{2,0,1:T(8,128)(2,1)S(1)}, s32[]{:T(128)}, /*index=5*/s32[]{:T(128)}) while((s32[]{:T(128)}, bf16[1,2816]{1,0:T(2,128)(2,1)S(1)}, s32[8,2]{0,1:T(2,128)S(1)}, bf16[8,1,384]{2,0,1:T(8,128)(2,1)S(1)}, s32[]{:T(128)}, /*index=5*/s32[]{:T(128)}) %tuple.115), condition=%wide.while_cond.1, body=%wide.while_body.1.sunk | while | flops 2 | bytes 3177 | solution.py:106
  155.2 3.5 %all-to-all-start.1 = ((bf16[1,8,2,384]{3,2,0,1:T(2,128)(2,1)}), bf16[1,8,2,384]{3,2,0,1:T(2,128)(2,1)S(1)}, u32[]{:S(2)}, u32[]{:S(2)}) async-start(bf16[1,8,2,384]{3,2,0,1:T(2,128)(2,1)} %copy.33), calls=%async_computation.1 | async-start | bytes 24576 | tf_op jit(solution)/shard_map/all_to_all | solution.py:116
  158.7 1.9 maximum_convert_fusion
  160.6 4.4 %all-to-all-done.1 = bf16[1,8,2,384]{3,2,0,1:T(2,128)(2,1)S(1)} async-done(((bf16[1,8,2,384]{3,2,0,1:T(2,128)(2,1)}), bf16[1,8,2,384]{3,2,0,1:T(2,128)(2,1)S(1)}, u32[]{:S(2)}, u32[]{:S(2)}) %all-to-all-start.1) | async-done | bytes 12320 | tf_op jit(solution)/shard_map/all_to_all | solution.py:116
  165.0 29.1 %while.42 = (s32[]{:T(128)}, f32[1,256,512]{2,1,0:T(8,128)}, bf16[2,1,8,384]{3,2,0,1:T(8,128)(2,1)S(1)}, bf16[2,8,512,128]{3,2,1,0:T(8,128)(2,1)}, s32[]{:T(128)}, /*index=5*/s32[]{:T(128)}) while((s32[]{:T(128)}, f32[1,256,512]{2,1,0:T(8,128)}, bf16[2,1,8,384]{3,2,0,1:T(8,128)(2,1)S(1)}, bf16[2,8,512,128]{3,2,1,0:T(8,128)(2,1)}, ...), condition=%wide.region_7.8_spmd.clone, body=%wide.region_6.7_spmd.clone.sunk | while | flops 301471744 | bytes 67193432 | solution.py:131
  167.1 1.1 maximum_select_fusion.34
  176.3 0.9 slice.383
  177.2 2.3 %fusion.41 = f32[1,256,512]{2,1,0:T(8,128)} fusion(bf16[2,8,512,128]{3,2,1,0:T(8,128)(2,1)S(1)} %copy-done, s32[]{:T(128)} %get-tuple-element.503, bf16[1,8,256,128]{3,2,1,0:T(8,128)(2,1)} %slice.383, bf16[1,8,256,256]{3,2,1,0:T(8,128)(2,1)S(1)} %slice.384, f32[1,256,512]{2,1,0:T(8,128)} %get-tuple-element.504, ...), kind=kOutput, calls=%fused_computation.42.clone.1 | convolution fusion | flops 270008320 | bytes 3670533 | tf_op jit(solution)/shard_map/while/body/eval_jaxpr/ytid,tzd->yiz/dot_general | solution.py:125
  181.6 1.1 maximum_select_fusion.34
  190.8 0.9 slice.383
  191.7 2.5 %fusion.41 = f32[1,256,512]{2,1,0:T(8,128)} fusion(bf16[2,8,512,128]{3,2,1,0:T(8,128)(2,1)S(1)} %copy-done, s32[]{:T(128)} %get-tuple-element.503, bf16[1,8,256,128]{3,2,1,0:T(8,128)(2,1)} %slice.383, bf16[1,8,256,256]{3,2,1,0:T(8,128)(2,1)S(1)} %slice.384, f32[1,256,512]{2,1,0:T(8,128)} %get-tuple-element.504, ...), kind=kOutput, calls=%fused_computation.42.clone.1 | convolution fusion | flops 270008320 | bytes 3670533 | tf_op jit(solution)/shard_map/while/body/eval_jaxpr/ytid,tzd->yiz/dot_general | solution.py:125
  194.2 2.8 %fusion.19 = f32[1,256,512]{2,1,0:T(8,128)} fusion(f32[1,256,514]{2,1,0:T(8,128)} %maximum_convert_fusion, f32[1,256,512]{2,1,0:T(8,128)} %param.12, f32[1,256,512]{2,1,0:T(8,128)} %get-tuple-element.161, f32[256,512]{1,0:T(8,128)} %param.15), kind=kLoop, calls=%fused_computation.65 | loop fusion | flops 917504 | bytes 3145728 | tf_op jit(solution)/shard_map/add | solution.py:134
  (271 shorter events, 65.8 us)
Async XLA Ops:
  6.5 55.0 %all-gather.2.cloned.1.call-start = ((), (), s32[]{:S(2)}) async-start(), calls=%async_computation.2 | async-start | bytes 2359296 | tf_op jit(solution)/shard_map/all_gather | solution.py:70
  9.0 149.7 %collective-permute-start = (bf16[1,256,1]{2,1,0:T(8,128)(2,1)}, bf16[1,256,1]{2,1,0:T(8,128)(2,1)}, u32[]{:S(2)}, u32[]{:S(2)}) collective-permute-start(bf16[1,256,1]{2,1,0:T(8,128)(2,1)} %get-tuple-element.283), channel_id=1, source_target_pairs={{0,1},{1,2},{2,3},{4,5},{5,6},{6,7},{8,9},{9,10},{10,11},{12,13},{... | collective-permute-start | bytes 1544 | tf_op jit(solution)/shard_map/ppermute | solution.py:19
  12.0 146.7 %collective-permute-start.1 = (bf16[1,256,1]{2,1,0:T(8,128)(2,1)}, bf16[1,256,1]{2,1,0:T(8,128)(2,1)}, u32[]{:S(2)}, u32[]{:S(2)}) collective-permute-start(bf16[1,256,1]{2,1,0:T(8,128)(2,1)} %get-tuple-element.284), channel_id=1, source_target_pairs={{1,0},{2,1},{3,2},{5,4},{6,5},{7,6},{9,8},{10,9},{11,10},{13,12},{... | collective-permute-start | bytes 1544 | tf_op jit(solution)/shard_map/ppermute | solution.py:21
  14.2 0.6 copy-start.1
  61.5 18.3 %copy-start.5 = (s32[8]{0:T(128)S(1)}, s32[8]{0:T(128)}, u32[]{:S(2)}) copy-start(s32[8]{0:T(128)} %get-tuple-element.237) | copy-start | bytes 100
  61.5 18.3 %copy-start.6 = (s32[8]{0:T(128)S(1)}, s32[8]{0:T(128)}, u32[]{:S(2)}) copy-start(s32[8]{0:T(128)} %get-tuple-element.238) | copy-start | bytes 100
  61.5 18.3 %copy-start.2 = (s32[2,8]{0,1:T(8,128)S(1)}, s32[2,8]{0,1:T(8,128)}, u32[]{:S(2)}) copy-start(s32[2,8]{0,1:T(8,128)} %copy-done.1) | copy-start | bytes 196
  61.5 70.4 %copy-start.3 = (f32[2,2816]{1,0:T(2,128)S(1)}, f32[2,2816]{1,0:T(2,128)}, u32[]{:S(2)}) copy-start(f32[2,2816]{1,0:T(2,128)} %param.14) | copy-start | bytes 67588
  61.5 70.4 %copy-start.4 = (f32[1,2,2816]{2,1,0:T(2,128)S(1)}, f32[1,2,2816]{2,1,0:T(2,128)}, u32[]{:S(2)}) copy-start(f32[1,2,2816]{2,1,0:T(2,128)} %param.13) | copy-start | bytes 67588
  76.4 9.9 %all-to-all-start = ((f32[8,2,1,384]{3,2,1,0:T(1,128)}), f32[8,2,1,384]{3,2,1,0:T(1,128)S(1)}, u32[]{:S(2)}, u32[]{:S(2)}) async-start(f32[8,2,1,384]{3,2,1,0:T(1,128)} %bitcast.12), calls=%async_computation | async-start | bytes 49152 | tf_op jit(solution)/shard_map/all_to_all | solution.py:93
  155.2 9.8 %all-to-all-start.1 = ((bf16[1,8,2,384]{3,2,0,1:T(2,128)(2,1)}), bf16[1,8,2,384]{3,2,0,1:T(2,128)(2,1)S(1)}, u32[]{:S(2)}, u32[]{:S(2)}) async-start(bf16[1,8,2,384]{3,2,0,1:T(2,128)(2,1)} %copy.33), calls=%async_computation.1 | async-start | bytes 24576 | tf_op jit(solution)/shard_map/all_to_all | solution.py:116
  175.5 1.7 copy-start
  190.0 1.7 copy-start
Sparse Core Ops, SparseCore 0:
  9.5 51.9 all-gather.1
where the time goes:
time: 205 us; the launch traced here: 204 us
  waiting for transfers between devices  57.6 us (28%)
  local copies, waits for them, and re-layouts  49.3 us (24%)
  loops' own time  28.2 us (14%)
  other arithmetic  25.6 us (12%)
  between operations  13.6 us (7%)
  starting transfers between devices  11.1 us (5%)
  blocking collectives  10.3 us (5%)
  matrix products  8.25 us (4%)
    all_gather x1, waiting for transfers between devices, per_device(): all_weights = lax.all_gather(band_weight, 'blk', axis=0, tiled=True)  46 us
    another operation x1, loops' own time, per_device(): partial_sum = lax.fori_loop(0, block_count, add_source, initial)  27.2 us
    gather x64, local copies, waits for them, and re-layouts  22.3 us
    select_n x28, other arithmetic, shift_rows(): rows = jnp.where(chosen, moved, rows)  16.4 us
    slice x60, local copies, waits for them, and re-layouts, shift_rows(): moved = jnp.roll(rows, direction * (1 << level), axis=-1)  15.1 us
    psum x1, blocking collectives, per_device(): projection = lax.psum(partial_sum, 'gy')  10.3 us
    all_to_all x1, waiting for transfers between devices, per_device(): lax.all_to_all(windows, 'blk', split_axis=0, concat_axis=0, tiled=True)  6.42 us
    dot_general x2, matrix products, back_group(): jnp.einsum('ytid,tzd->yiz', sheared, weight_part, preferred_element_type=...  4.81 us
  transfers between devices with their start and end apart: 5, of which 3 were waited for; matrix products, arithmetic and copies ran while one was open for 25% of the time, Pallas kernels for 0%

commit v1 on v0

--- a/solution.py
+++ b/solution.py
@@ -6,6 +6,28 @@
 
 PW = 128
 SMOOTH = 0.25
+
+
+def cut_along(array, dim, peers):
+    before, after = (array.shape[:dim], array.shape[dim + 1 :])
+    return jnp.moveaxis(array.reshape(*before, peers, -1, *after), dim, 0)
+
+
+def joined_along(tiles, dim):
+    tiles = jnp.moveaxis(tiles, 0, dim)
+    lengths = tiles.shape
+    return tiles.reshape(*lengths[:dim], lengths[dim] * lengths[dim + 1], *lengths[dim + 2 :])
+
+
+def exchange_in_pairs(array, axis, split_dim, concat_dim):
+    size, here = (lax.axis_size(axis), lax.axis_index(axis))
+    blocks = cut_along(array, split_dim, size)
+    outs = [blocks[here]]
+    for step in range(1, size):
+        sent = blocks[here ^ step]
+        outs.append(lax.ppermute(sent, axis, [(i, i ^ step) for i in range(size)]))
+    blocks = jnp.stack(outs)[here ^ jnp.arange(size)]
+    return joined_along(blocks, concat_dim)
 
 
 def with_halo(cells, sides, width):
@@ -90,7 +112,7 @@
 
     windows = lax.map(project_group, weight_groups)
     windows = windows.reshape(block_count, local_tilts, row_count, window_len)
-    received = lax.all_to_all(windows, "blk", split_axis=0, concat_axis=0, tiled=True)
+    received = exchange_in_pairs(windows, "blk", 0, 0)
 
     def add_source(source, running):
         return place_windows(

time: 205 us -> 213 us (1.039)
  starting transfers between devices: 11.1 us -> 19.3 us
  loops' own time: 28.2 us -> 31.7 us
  waiting for transfers between devices: 57.6 us -> 54.8 us
    ppermute x0 -> x7, starting transfers between devices: none -> 11.4 us  [exchange_in_pairs(): outs.append(lax.ppermute(sent, axis, [(i, i ^ step) for i in range(size)]))]
    all_to_all x1 -> x0, waiting for transfers between devices: 6.42 us -> none  [per_device(): lax.all_to_all(windows, 'blk', split_axis=0, concat_axis=0, tiled=True)]
    ppermute x0 -> x7, waiting for transfers between devices: none -> 3.93 us  [exchange_in_pairs(): outs.append(lax.ppermute(sent, axis, [(i, i ^ step) for i in range(size)]))]
    another operation x1, loops' own time: 27.2 us -> 30.6 us  [per_device(): partial_sum = lax.fori_loop(0, block_count, add_source, initial)]
    all_to_all x1 -> x0, starting transfers between devices: 3.34 us -> none  [per_device(): lax.all_to_all(windows, 'blk', split_axis=0, concat_axis=0, tiled=True)]
    gather x64 -> x65, local copies, waits for them, and re-layouts: 22.3 us -> 21.5 us
  transfers between devices with their start and end apart: 5 -> 11, of which waited for: 3 -> 4; matrix products, arithmetic and copies ran while one was open for 25% -> 24% of each run, Pallas kernels for 0% -> 0%
where the time goes in v1:
time: 213 us; the launch traced here: 212 us
  waiting for transfers between devices  54.8 us (26%)
  local copies, waits for them, and re-layouts  47.3 us (22%)
  loops' own time  31.7 us (15%)
  other arithmetic  26.7 us (13%)
  starting transfers between devices  19.3 us (9%)
  between operations  13.7 us (6%)
  blocking collectives  10.3 us (5%)
  matrix products  8.24 us (4%)
    all_gather x1, waiting for transfers between devices, per_device(): all_weights = lax.all_gather(band_weight, 'blk', axis=0, tiled=True)  45.5 us
    another operation x1, loops' own time, per_device(): partial_sum = lax.fori_loop(0, block_count, add_source, initial)  30.6 us
    gather x64, local copies, waits for them, and re-layouts  20.9 us
    select_n x28, other arithmetic, shift_rows(): rows = jnp.where(chosen, moved, rows)  16.4 us
    slice x60, local copies, waits for them, and re-layouts, shift_rows(): moved = jnp.roll(rows, direction * (1 << level), axis=-1)  15.1 us
    ppermute x7, starting transfers between devices, exchange_in_pairs(): outs.append(lax.ppermute(sent, axis, [(i, i ^ step) for i in range(size)]))  11.4 us
    psum x1, blocking collectives, per_device(): projection = lax.psum(partial_sum, 'gy')  10.3 us
    dynamic_slice x8, local copies, waits for them, and re-layouts, place_windows(): offset = own_bins[tilt_slot, source]  5.15 us
  transfers between devices with their start and end apart: 11, of which 4 were waited for; matrix products, arithmetic and copies ran while one was open for 24% of the time, Pallas kernels for 0%

profile of v1, /device:TPU:0, one launch (start us, length us, event | category | flops | bytes accessed | tf_op | source)
XLA Modules:
  0.0 211.9 jit_solution(9157304032204798938)
XLA Ops:
  9.0 3.0 %collective-permute-start.7 = (bf16[1,256,1]{2,1,0:T(8,128)(2,1)}, bf16[1,256,1]{2,1,0:T(8,128)(2,1)}, u32[]{:S(2)}, u32[]{:S(2)}) collective-permute-start(bf16[1,256,1]{2,1,0:T(8,128)(2,1)} %get-tuple-element.283), channel_id=1, source_target_pairs={{0,1},{1,2},{2,3},{4,5},{5,6},{6,7},{8,9},{9,10},{10,11},{12,13},{... | collective-permute-start | bytes 1544 | tf_op jit(solution)/shard_map/ppermute | solution.py:41
  12.0 1.3 collective-permute-start.8
  16.1 45.5 %all-gather.2.cloned.1.call-done = bf16[16,512,128]{2,1,0:T(8,128)(2,1)} async-done(((bf16[2,512,128]{2,1,0:T(8,128)(2,1)}), bf16[16,512,128]{2,1,0:T(8,128)(2,1)}) %all-gather.2.cloned.1.call-update) | async-done | bytes 2097168 | tf_op jit(solution)/shard_map/all_gather | solution.py:92
  61.6 13.7 %while.38 = (s32[]{:T(128)}, f32[2,8,1,384]{3,2,1,0:T(1,128)S(1)}, bf16[2,8,512,128]{3,2,1,0:T(8,128)(2,1)}, bf16[1,256,512]{2,1,0:T(8,128)(2,1)S(1)}, s32[]{:T(128)}) while((s32[]{:T(128)}, f32[2,8,1,384]{3,2,1,0:T(1,128)S(1)}, bf16[2,8,512,128]{3,2,1,0:T(8,128)(2,1)}, bf16[1,256,512]{2,1,0:T(8,128)(2,1)S(1)}, s32[]{:T(128)}) %tuple.133), condition=%wide.region_2.3_spmd, body=%wide.region_0.2_spmd.sunk | while | flops 281021440 | bytes 108388928 | solution.py:113
  61.7 1.7 convolution_bitcast_fusion.3
  68.5 1.7 convolution_bitcast_fusion.3
  76.2 1.6 collective-permute-start.1
  77.8 1.4 collective-permute-start.2
  79.2 1.8 collective-permute-start.3
  81.0 1.6 collective-permute-start.4
  82.6 2.0 collective-permute-start.5
  84.6 2.4 %collective-permute-start.6 = (f32[1,2,1,384]{3,2,1,0:T(1,128)S(1)}, f32[1,2,1,384]{3,2,1,0:T(1,128)S(1)}, u32[]{:S(2)}, u32[]{:S(2)}) collective-permute-start(f32[1,2,1,384]{3,2,1,0:T(1,128)S(1)} %get-tuple-element.285), channel_id=1, source_target_pairs={{0,28},{4,24},{8,20},{12,16},{16,12},{20,8},{24,4},{28,0},{1,29},{... | collective-permute-start | bytes 9224 | tf_op jit(solution)/shard_map/ppermute | solution.py:28
  88.0 2.9 %collective-permute-done.6 = f32[1,2,1,384]{3,2,1,0:T(1,128)S(1)} collective-permute-done((f32[1,2,1,384]{3,2,1,0:T(1,128)S(1)}, f32[1,2,1,384]{3,2,1,0:T(1,128)S(1)}, u32[]{:S(2)}, u32[]{:S(2)}) %collective-permute-start.6) | collective-permute-done | bytes 3104 | tf_op jit(solution)/shard_map/ppermute | solution.py:28
  91.6 39.2 %while.39 = (s32[]{:T(128)}, f32[1,2,2816]{2,1,0:T(2,128)S(1)}, s32[2,8]{1,0:T(2,128)S(1)}, f32[8,2,1,384]{3,2,1,0:T(1,128)S(1)}, s32[]{:T(128)}, /*index=5*/s32[]{:T(128)}, s32[]{:T(128)}, s32[]{}) while((s32[]{:T(128)}, f32[1,2,2816]{2,1,0:T(2,128)S(1)}, s32[2,8]{1,0:T(2,128)S(1)}, f32[8,2,1,384]{3,2,1,0:T(1,128)S(1)}, s32[]{:T(128)}, ...), condition=%wide.region_4.5_spmd, body=%wide.region_3.4_spmd.sunk | while | flops 777 | bytes 15573 | solution.py:122
  130.8 10.3 %psum.7 = f32[1,2,2816]{2,1,0:T(2,128)S(1)} all-reduce(f32[1,2,2816]{2,1,0:T(2,128)S(1)} %get-tuple-element.160), channel_id=1, replica_groups=mesh['blk'=8,'gy'=4] {'gy'}, use_global_device_ids=true, to_apply=%region_5.6 | all-reduce | flops 5632 | bytes 45056 | tf_op jit(solution)/shard_map/psum | solution.py:123
  141.1 10.9 %while.40 = (s32[]{:T(128)}, bf16[1,2816]{1,0:T(2,128)(2,1)S(1)}, s32[8,2]{0,1:T(2,128)S(1)}, bf16[8,1,384]{2,0,1:T(8,128)(2,1)S(1)}, s32[]{:T(128)}, /*index=5*/s32[]{:T(128)}) while((s32[]{:T(128)}, bf16[1,2816]{1,0:T(2,128)(2,1)S(1)}, s32[8,2]{0,1:T(2,128)S(1)}, bf16[8,1,384]{2,0,1:T(8,128)(2,1)S(1)}, s32[]{:T(128)}, /*index=5*/s32[]{:T(128)}) %tuple.125), condition=%wide.while_cond, body=%wide.while_body.sunk | while | flops 2 | bytes 3177 | solution.py:128
  152.1 10.2 %while.41 = (s32[]{:T(128)}, bf16[1,2816]{1,0:T(2,128)(2,1)S(1)}, s32[8,2]{0,1:T(2,128)S(1)}, bf16[8,1,384]{2,0,1:T(8,128)(2,1)S(1)}, s32[]{:T(128)}, /*index=5*/s32[]{:T(128)}) while((s32[]{:T(128)}, bf16[1,2816]{1,0:T(2,128)(2,1)S(1)}, s32[8,2]{0,1:T(2,128)S(1)}, bf16[8,1,384]{2,0,1:T(8,128)(2,1)S(1)}, s32[]{:T(128)}, /*index=5*/s32[]{:T(128)}) %tuple.122), condition=%wide.while_cond.1, body=%wide.while_body.1.sunk | while | flops 2 | bytes 3177 | solution.py:128
  162.9 3.6 %all-to-all-start = ((bf16[1,8,2,384]{3,2,0,1:T(2,128)(2,1)}), bf16[1,8,2,384]{3,2,0,1:T(2,128)(2,1)S(1)}, u32[]{:S(2)}, u32[]{:S(2)}) async-start(bf16[1,8,2,384]{3,2,0,1:T(2,128)(2,1)} %copy.33), calls=%async_computation | async-start | bytes 24576 | tf_op jit(solution)/shard_map/all_to_all | solution.py:138
  166.5 1.9 maximum_convert_fusion
  168.4 4.6 %all-to-all-done = bf16[1,8,2,384]{3,2,0,1:T(2,128)(2,1)S(1)} async-done(((bf16[1,8,2,384]{3,2,0,1:T(2,128)(2,1)}), bf16[1,8,2,384]{3,2,0,1:T(2,128)(2,1)S(1)}, u32[]{:S(2)}, u32[]{:S(2)}) %all-to-all-start) | async-done | bytes 12320 | tf_op jit(solution)/shard_map/all_to_all | solution.py:138
  173.0 29.1 %while.42 = (s32[]{:T(128)}, f32[1,256,512]{2,1,0:T(8,128)}, bf16[2,1,8,384]{3,2,0,1:T(8,128)(2,1)S(1)}, bf16[2,8,512,128]{3,2,1,0:T(8,128)(2,1)}, s32[]{:T(128)}, /*index=5*/s32[]{:T(128)}) while((s32[]{:T(128)}, f32[1,256,512]{2,1,0:T(8,128)}, bf16[2,1,8,384]{3,2,0,1:T(8,128)(2,1)S(1)}, bf16[2,8,512,128]{3,2,1,0:T(8,128)(2,1)}, ...), condition=%wide.region_7.8_spmd.clone, body=%wide.region_6.7_spmd.clone.sunk | while | flops 301471744 | bytes 67193432 | solution.py:153
  185.2 2.3 %fusion.42 = f32[1,256,512]{2,1,0:T(8,128)} fusion(bf16[2,8,512,128]{3,2,1,0:T(8,128)(2,1)S(1)} %copy-done, s32[]{:T(128)} %get-tuple-element.511, bf16[1,8,256,128]{3,2,1,0:T(8,128)(2,1)} %slice.385, bf16[1,8,256,256]{3,2,1,0:T(8,128)(2,1)S(1)} %slice.386, f32[1,256,512]{2,1,0:T(8,128)} %get-tuple-element.512, ...), kind=kOutput, calls=%fused_computation.43.clone.1 | convolution fusion | flops 270008320 | bytes 3670533 | tf_op jit(solution)/shard_map/while/body/eval_jaxpr/ytid,tzd->yiz/dot_general | solution.py:147
  199.7 2.5 %fusion.42 = f32[1,256,512]{2,1,0:T(8,128)} fusion(bf16[2,8,512,128]{3,2,1,0:T(8,128)(2,1)S(1)} %copy-done, s32[]{:T(128)} %get-tuple-element.511, bf16[1,8,256,128]{3,2,1,0:T(8,128)(2,1)} %slice.385, bf16[1,8,256,256]{3,2,1,0:T(8,128)(2,1)S(1)} %slice.386, f32[1,256,512]{2,1,0:T(8,128)} %get-tuple-element.512, ...), kind=kOutput, calls=%fused_computation.43.clone.1 | convolution fusion | flops 270008320 | bytes 3670533 | tf_op jit(solution)/shard_map/while/body/eval_jaxpr/ytid,tzd->yiz/dot_general | solution.py:147
  202.2 2.8 %fusion.19 = f32[1,256,512]{2,1,0:T(8,128)} fusion(f32[1,256,514]{2,1,0:T(8,128)} %maximum_convert_fusion, f32[1,256,512]{2,1,0:T(8,128)} %param.12, f32[1,256,512]{2,1,0:T(8,128)} %get-tuple-element.161, f32[256,512]{1,0:T(8,128)} %param.15), kind=kLoop, calls=%fused_computation.66 | loop fusion | flops 917504 | bytes 3145728 | tf_op jit(solution)/shard_map/add | solution.py:156
  (298 shorter events, 71.6 us)
Async XLA Ops:
  6.5 55.1 %all-gather.2.cloned.1.call-start = ((), (), s32[]{:S(2)}) async-start(), calls=%async_computation.1 | async-start | bytes 2359296 | tf_op jit(solution)/shard_map/all_gather | solution.py:92
  9.0 157.4 %collective-permute-start.7 = (bf16[1,256,1]{2,1,0:T(8,128)(2,1)}, bf16[1,256,1]{2,1,0:T(8,128)(2,1)}, u32[]{:S(2)}, u32[]{:S(2)}) collective-permute-start(bf16[1,256,1]{2,1,0:T(8,128)(2,1)} %get-tuple-element.283), channel_id=1, source_target_pairs={{0,1},{1,2},{2,3},{4,5},{5,6},{6,7},{8,9},{9,10},{10,11},{12,13},{... | collective-permute-start | bytes 1544 | tf_op jit(solution)/shard_map/ppermute | solution.py:41
  12.0 154.5 %collective-permute-start.8 = (bf16[1,256,1]{2,1,0:T(8,128)(2,1)}, bf16[1,256,1]{2,1,0:T(8,128)(2,1)}, u32[]{:S(2)}, u32[]{:S(2)}) collective-permute-start(bf16[1,256,1]{2,1,0:T(8,128)(2,1)} %get-tuple-element.284), channel_id=1, source_target_pairs={{1,0},{2,1},{3,2},{5,4},{6,5},{7,6},{9,8},{10,9},{11,10},{13,12},{... | collective-permute-start | bytes 1544 | tf_op jit(solution)/shard_map/ppermute | solution.py:43
  14.7 0.6 copy-start.1
  61.6 14.4 %copy-start.7 = (s32[8]{0:T(128)S(1)}, s32[8]{0:T(128)}, u32[]{:S(2)}) copy-start(s32[8]{0:T(128)} %fusion.22) | copy-start | bytes 100
  61.6 14.5 %copy-start.2 = (s32[2,8]{0,1:T(8,128)S(1)}, s32[2,8]{0,1:T(8,128)}, u32[]{:S(2)}) copy-start(s32[2,8]{0,1:T(8,128)} %copy-done.1) | copy-start | bytes 196
  61.6 14.5 %copy-start.6 = (s32[8,1]{0,1:T(1,128)S(1)}, s32[8,1]{0,1:T(1,128)}, u32[]{:S(2)}) copy-start(s32[8,1]{0,1:T(1,128)} %get-tuple-element.296) | copy-start | bytes 100
  61.6 14.6 %copy-start.5 = (s32[8,1]{0,1:T(1,128)S(1)}, s32[8,1]{0,1:T(1,128)}, u32[]{:S(2)}) copy-start(s32[8,1]{0,1:T(1,128)} %get-tuple-element.295) | copy-start | bytes 100
  61.6 79.4 %copy-start.3 = (f32[2,2816]{1,0:T(2,128)S(1)}, f32[2,2816]{1,0:T(2,128)}, u32[]{:S(2)}) copy-start(f32[2,2816]{1,0:T(2,128)} %param.14) | copy-start | bytes 67588
  61.6 79.4 %copy-start.4 = (f32[1,2,2816]{2,1,0:T(2,128)S(1)}, f32[1,2,2816]{2,1,0:T(2,128)}, u32[]{:S(2)}) copy-start(f32[1,2,2816]{2,1,0:T(2,128)} %param.13) | copy-start | bytes 67588
  75.4 3.8 %collective-permute-start = (f32[1,2,1,384]{3,2,1,0:T(1,128)S(1)}, f32[1,2,1,384]{3,2,1,0:T(1,128)S(1)}, u32[]{:S(2)}, u32[]{:S(2)}) collective-permute-start(f32[1,2,1,384]{3,2,1,0:T(1,128)S(1)} %get-tuple-element.291), channel_id=1, source_target_pairs={{0,4},{4,0},{8,12},{12,8},{16,20},{20,16},{24,28},{28,24},{1,5},{5... | collective-permute-start | bytes 9224 | tf_op jit(solution)/shard_map/ppermute | solution.py:28
  76.2 4.8 %collective-permute-start.1 = (f32[1,2,1,384]{3,2,1,0:T(1,128)S(1)}, f32[1,2,1,384]{3,2,1,0:T(1,128)S(1)}, u32[]{:S(2)}, u32[]{:S(2)}) collective-permute-start(f32[1,2,1,384]{3,2,1,0:T(1,128)S(1)} %get-tuple-element.290), channel_id=1, source_target_pairs={{0,8},{4,12},{8,0},{12,4},{16,24},{20,28},{24,16},{28,20},{1,9},{5... | collective-permute-start | bytes 9224 | tf_op jit(solution)/shard_map/ppermute | solution.py:28
  77.8 4.9 %collective-permute-start.2 = (f32[1,2,1,384]{3,2,1,0:T(1,128)S(1)}, f32[1,2,1,384]{3,2,1,0:T(1,128)S(1)}, u32[]{:S(2)}, u32[]{:S(2)}) collective-permute-start(f32[1,2,1,384]{3,2,1,0:T(1,128)S(1)} %get-tuple-element.289), channel_id=1, source_target_pairs={{0,12},{4,8},{8,4},{12,0},{16,28},{20,24},{24,20},{28,16},{1,13},{... | collective-permute-start | bytes 9224 | tf_op jit(solution)/shard_map/ppermute | solution.py:28
  79.2 5.4 %collective-permute-start.3 = (f32[1,2,1,384]{3,2,1,0:T(1,128)S(1)}, f32[1,2,1,384]{3,2,1,0:T(1,128)S(1)}, u32[]{:S(2)}, u32[]{:S(2)}) collective-permute-start(f32[1,2,1,384]{3,2,1,0:T(1,128)S(1)} %get-tuple-element.288), channel_id=1, source_target_pairs={{0,16},{4,20},{8,24},{12,28},{16,0},{20,4},{24,8},{28,12},{1,17},{... | collective-permute-start | bytes 9224 | tf_op jit(solution)/shard_map/ppermute | solution.py:28
  81.0 6.0 %collective-permute-start.4 = (f32[1,2,1,384]{3,2,1,0:T(1,128)S(1)}, f32[1,2,1,384]{3,2,1,0:T(1,128)S(1)}, u32[]{:S(2)}, u32[]{:S(2)}) collective-permute-start(f32[1,2,1,384]{3,2,1,0:T(1,128)S(1)} %get-tuple-element.287), channel_id=1, source_target_pairs={{0,20},{4,16},{8,28},{12,24},{16,4},{20,0},{24,12},{28,8},{1,21},{... | collective-permute-start | bytes 9224 | tf_op jit(solution)/shard_map/ppermute | solution.py:28
  82.6 5.4 %collective-permute-start.5 = (f32[1,2,1,384]{3,2,1,0:T(1,128)S(1)}, f32[1,2,1,384]{3,2,1,0:T(1,128)S(1)}, u32[]{:S(2)}, u32[]{:S(2)}) collective-permute-start(f32[1,2,1,384]{3,2,1,0:T(1,128)S(1)} %get-tuple-element.286), channel_id=1, source_target_pairs={{0,24},{4,28},{8,16},{12,20},{16,8},{20,12},{24,0},{28,4},{1,25},{... | collective-permute-start | bytes 9224 | tf_op jit(solution)/shard_map/ppermute | solution.py:28
  84.6 6.3 %collective-permute-start.6 = (f32[1,2,1,384]{3,2,1,0:T(1,128)S(1)}, f32[1,2,1,384]{3,2,1,0:T(1,128)S(1)}, u32[]{:S(2)}, u32[]{:S(2)}) collective-permute-start(f32[1,2,1,384]{3,2,1,0:T(1,128)S(1)} %get-tuple-element.285), channel_id=1, source_target_pairs={{0,28},{4,24},{8,20},{12,16},{16,12},{20,8},{24,4},{28,0},{1,29},{... | collective-permute-start | bytes 9224 | tf_op jit(solution)/shard_map/ppermute | solution.py:28
  162.9 10.2 %all-to-all-start = ((bf16[1,8,2,384]{3,2,0,1:T(2,128)(2,1)}), bf16[1,8,2,384]{3,2,0,1:T(2,128)(2,1)S(1)}, u32[]{:S(2)}, u32[]{:S(2)}) async-start(bf16[1,8,2,384]{3,2,0,1:T(2,128)(2,1)} %copy.33), calls=%async_computation | async-start | bytes 24576 | tf_op jit(solution)/shard_map/all_to_all | solution.py:138
  183.5 1.7 copy-start
  198.0 1.7 copy-start
Sparse Core Ops, SparseCore 0:
  9.5 52.0 all-gather.1
